TPU v7x, 32 devices: a whole 2x2x4 slice. The times are simulated.
32 devices in a mesh: ctx: 8 (over z, x), head: 4 (over y, core).
Axes of the slice: x: 2, y: 2, z: 4, core: 2. Of those that a mesh axis runs over, the one named last changes fastest.
Arguments:
- queries: bfloat16 [8192, 1024], P('ctx', 'head'), may hold values from -6 to 6
- keys: bfloat16 [8192, 1024], P('ctx', 'head'), may hold values from -6 to 6
- values: bfloat16 [8192, 1024], P('ctx', 'head'), may hold values from -6 to 6
- level_index: int32 [8192], P('ctx'), may hold values from 0 to 15
- level_table: float32 [16, 8, 8], P(None, 'head'), may hold values from 0.2 to 2
- head_gain: float32 [1024], P('head'), may hold values from 0.5 to 1.5
- residual: bfloat16 [8192, 1024], P(('ctx', 'head')), may hold values from -6 to 6
- w_out: bfloat16 [1024, 1024], replicated, may hold values from -0.1875 to 0.1875
- norm_gain: float32 [1024], replicated, may hold values from 0.5 to 1.5
- w_qkv: bfloat16 [1024, 3072], replicated, may hold values from -8 to 8
- windows: int32 [8], replicated, may hold values from 64 to 256, as said below
Outputs:
- hidden: bfloat16 [8192, 1024], P(('ctx', 'head'))
- attended: bfloat16 [8192, 1024], P('ctx', 'head')
Inputs may be any that keep to these rules, and one draw needn't show every extreme that they name: `windows`: each head's key window; some head's window is exactly 256 in every draw.
All inputs are finite; a program needn't handle non-finite values.
Results may differ from a plain program's by a relative error of at most 0.014.
Values may be sent and summed in bfloat16 or wider, within the bound.
A program may use at most 128 MiB of HBM per device.

v0:
```python
import jax
import jax.numpy as jnp
from jax import lax
from jax.sharding import PartitionSpec as P

STRETCH = 64
WINDOW = 256


EPSILON = 1e-05
PRECISE = lax.Precision.HIGHEST


def from_behind(block, axis, distance):
    devices = range(lax.axis_size(axis))
    route = [(i - distance, i) for i in devices if i - distance in devices]
    return lax.ppermute(block, axis, route)


def bfloat(array):
    return array.astype(jnp.bfloat16)


def attend_block(
    query_block, key_block, value_block, head_windows, query_pos, key_pos, score_scale
):
    scores = (
        jnp.einsum("qhd,khd->hqk", query_block, key_block, preferred_element_type=jnp.float32)
        * score_scale
    )
    distance = query_pos[:, None] - key_pos[None, :]
    allowed = (
        (distance >= 0)[None]
        & (distance < head_windows[:, None, None])
        & (key_pos >= 0)[None, None, :]
    )
    scores = jnp.where(allowed, scores, -1e30)
    row_max = jnp.max(scores, -1, keepdims=True)
    weights = jnp.exp(scores - row_max)
    probs = bfloat(weights / jnp.sum(weights, -1, keepdims=True))
    return bfloat(
        jnp.einsum("hqk,khd->qhd", probs, value_block, preferred_element_type=jnp.float32)
    )


def windowed(query_rows, key_value, head_windows, first_pos, context_rows, score_scale):
    query_count = query_rows.shape[0]
    block_rows = min(query_count, 512)
    block_count = query_count // block_rows

    def attend_one(block_index):
        offset = block_index * block_rows
        query_pos = first_pos + offset + jnp.arange(block_rows, dtype=jnp.int32)
        key_pos = (
            first_pos
            + offset
            - context_rows
            + jnp.arange(context_rows + block_rows, dtype=jnp.int32)
        )
        return attend_block(
            query_rows,
            key_value[:, 0],
            key_value[:, 1],
            head_windows,
            query_pos,
            key_pos,
            score_scale,
        )

    results = lax.map(attend_one, jnp.arange(block_count, dtype=jnp.int32))
    return results.reshape((query_count,) + query_rows.shape[1:])


def per_device(
    queries,
    keys,
    values,
    level_index,
    level_table,
    head_gain,
    residual,
    w_out,
    norm_gain,
    w_qkv,
    windows,
):
    token_count = queries.shape[0]
    local_heads = level_table.shape[1]
    levels = level_table.shape[2]
    head_dim = head_gain.shape[0] // local_heads
    stretch_len = STRETCH
    stretches = token_count // stretch_len
    local_bits = stretches.bit_length() - 1
    ctx_bits = lax.axis_size("ctx").bit_length() - 1
    position = lax.axis_index("ctx")
    stretch_shape = (stretches, stretch_len, local_heads, head_dim)
    query_stretches = queries.reshape(stretch_shape)
    key_stretches = keys.reshape(stretch_shape)
    value_stretches = values.reshape(stretch_shape)
    states = jnp.einsum(
        "jchd,jche->jhde", key_stretches, value_stretches, preferred_element_type=jnp.float32
    )
    device_state = jnp.sum(states, 0).reshape(local_heads * head_dim, head_dim)
    piece = lax.all_gather(device_state[None], "ctx", axis=0, tiled=True)
    piece_rows = piece.shape[0]
    source = jnp.arange(piece_rows, dtype=jnp.int32)
    span_sizes = 2 ** jnp.arange(ctx_bits, dtype=jnp.int32)
    lower_edge = position // (2 * span_sizes) * (2 * span_sizes)
    upper_edge = position // span_sizes * span_sizes
    member = ((source[:, None] >= lower_edge[None]) & (source[:, None] < upper_edge[None])).astype(
        jnp.float32
    )
    remote = jnp.einsum("nb,nxy->bxy", member, piece, precision=PRECISE)
    level_rows = level_table.reshape(level_table.shape[0], local_heads * levels)
    onehot = (
        level_index[:, None] == jnp.arange(level_rows.shape[0], dtype=jnp.int32)[None]
    ).astype(jnp.float32)
    level_weight = jnp.dot(onehot, level_rows, precision=PRECISE).reshape(
        stretches, stretch_len, local_heads, levels
    )
    causal = (
        jnp.arange(stretch_len, dtype=jnp.int32)[:, None]
        >= jnp.arange(stretch_len, dtype=jnp.int32)[None, :]
    )
    scores = jnp.einsum(
        "jthd,jshd->jhts", query_stretches, key_stretches, preferred_element_type=jnp.float32
    )
    scores = bfloat(jnp.where(causal[None, None], scores, 0.0))
    inside = jnp.einsum(
        "jhts,jshd->jthd", scores, value_stretches, preferred_element_type=jnp.float32
    )
    running = level_weight[..., 0:1] * stretch_len ** (-0.5) * inside
    for level_bit in range(local_bits):
        block_len = 2**level_bit
        group_total = stretches // block_len
        grouped = jnp.sum(
            states.reshape(group_total, block_len, local_heads, head_dim, head_dim), 1
        )
        earlier = jnp.concatenate([jnp.zeros_like(grouped[:1]), grouped[:-1]], 0)
        odd_mask = (jnp.arange(group_total, dtype=jnp.int32) % 2).astype(jnp.float32)
        read_state = bfloat(earlier * odd_mask[:, None, None, None])
        blocked_query = query_stretches.reshape(
            group_total, block_len * stretch_len, local_heads, head_dim
        )
        part_sum = jnp.einsum(
            "mthd,mhde->mthe", blocked_query, read_state, preferred_element_type=jnp.float32
        )
        weight_now = level_weight[..., 1 + level_bit : 2 + level_bit] * (
            stretch_len * block_len
        ) ** (-0.5)
        running = running + weight_now * part_sum.reshape(stretch_shape)
    remote_read = bfloat(remote.reshape(ctx_bits, local_heads, head_dim, head_dim))
    flat_query = queries.reshape(token_count, local_heads, head_dim)
    far_terms = jnp.einsum(
        "thd,bhde->tbhe", flat_query, remote_read, preferred_element_type=jnp.float32
    )
    far_rates = jnp.array(
        [(stretch_len * 2 ** (local_bits + level_bit)) ** (-0.5) for level_bit in range(ctx_bits)],
        jnp.float32,
    )
    far_weights = (
        level_weight.reshape(token_count, local_heads, levels)[:, :, 1 + local_bits :] * far_rates
    )
    running = running.reshape(token_count, local_heads, head_dim) + jnp.einsum(
        "tbhe,thb->the", far_terms, far_weights, precision=PRECISE
    )
    mean_square = jnp.mean(running * running, -1, keepdims=True)
    heads_out = bfloat(
        running * lax.rsqrt(mean_square + EPSILON) * head_gain.reshape(local_heads, head_dim)
    )
    group_count = lax.axis_size("head")
    row_count = token_count // group_count
    sectioned = heads_out.reshape(group_count, row_count, local_heads * head_dim)
    projected = jnp.einsum(
        "grc,cd->grd",
        lax.all_to_all(sectioned, "head", split_axis=0, concat_axis=2, tiled=True),
        w_out,
        preferred_element_type=jnp.float32,
    )
    hidden = bfloat(residual.astype(jnp.float32) + projected[0])
    hidden_f = hidden.astype(jnp.float32)
    normed = bfloat(
        hidden_f * lax.rsqrt(jnp.mean(hidden_f * hidden_f, -1, keepdims=True) + EPSILON) * norm_gain
    )
    projected_qkv = bfloat(jnp.dot(normed, w_qkv, preferred_element_type=jnp.float32))
    heads_total = w_qkv.shape[1] // (3 * head_dim)
    score_scale = head_dim ** (-0.5)
    local_qkv = projected_qkv.reshape(row_count, 3, heads_total, head_dim)
    tail_len = min(row_count, WINDOW)
    need_count = (WINDOW - 1 + row_count - 1) // row_count
    tail_pairs = local_qkv[row_count - tail_len :, 1:3]
    before = [from_behind(tail_pairs, ("ctx", "head"), 1)]
    key_value = jnp.concatenate(before + [local_qkv[:, 1:3]], 0)
    first_pos = position * token_count + lax.axis_index("head") * row_count
    result = windowed(
        local_qkv[:, 0], key_value, windows, first_pos, need_count * tail_len, score_scale
    )
    spread = result.reshape(row_count, group_count, local_heads * head_dim)
    gathered_out = lax.all_to_all(spread, "head", split_axis=1, concat_axis=0, tiled=True)
    return (hidden, gathered_out.reshape(token_count, local_heads * head_dim))


def solution(mesh):
    in_specs = (
        P("ctx", "head"),
        P("ctx", "head"),
        P("ctx", "head"),
        P("ctx"),
        P(None, "head", None),
        P("head"),
        P(("ctx", "head"), None),
        P(),
        P(),
        P(),
        P(),
    )
    out_specs = (P(("ctx", "head"), None), P("ctx", "head"))
    return jax.shard_map(
        per_device, mesh=mesh, in_specs=in_specs, out_specs=out_specs, check_vma=False
    )
```

profile of v0, /device:TPU:0, one launch (start us, length us, event | category | flops | bytes accessed | tf_op | source)
XLA Modules:
  0.0 138.8 jit_solution(12786850182399297132)
XLA Ops:
  10.6 2.5 %fusion.81 = (f32[2,128,128]{2,1,0:T(8,128)}, f32[16,2,128,128]{3,2,1,0:T(8,128)}) fusion(bf16[16,64,2,128]{3,2,1,0:T(2,128)(2,1)S(1)} %reshape.265, bf16[16,64,2,128]{3,2,1,0:T(2,128)(2,1)S(1)} %reshape.264), kind=kOutput, calls=%fused_computation.139 | convolution fusion | flops 67600384 | bytes 3276800 | tf_op jit(solution)/shard_map/jchd,jche->jhde/dot_general | solution.py:100
  13.1 3.0 %bitcast_reduce_fusion.2 = f32[8,2,128,128]{3,2,1,0:T(8,128)} fusion(f32[16,2,128,128]{3,2,1,0:T(8,128)} %get-tuple-element.26), kind=kLoop, calls=%fused_computation.10 | loop fusion | flops 262144 | bytes 3145728 | tf_op jit(solution)/shard_map/reduce_sum | solution.py:136
  18.8 1.8 %fusion.35 = f32[1024,16]{0,1:T(8,128)} fusion(s32[1024]{0:T(1024)} %param.15, f32[16,2,8]{0,2,1:T(8,128)S(1)} %copy-done.17), kind=kOutput, calls=%fused_computation.65 | convolution fusion | flops 3162112 | bytes 70656 | tf_op jit(solution)/shard_map/dot_general | solution.py:118
  20.6 1.6 %reshape.262 = f32[16,64,2,8]{1,0,3,2:T(8,128)} reshape(f32[1024,16]{0,1:T(8,128)} %fusion.35) | data formatting | bytes 131072 | tf_op jit(solution)/shard_map/reshape | solution.py:118
  22.2 2.1 %slice-done = f32[7,2,128,128]{3,2,1,0:T(8,128)S(1)} async-done(((f32[8,2,128,128]{3,2,1,0:T(8,128)}), f32[7,2,128,128]{3,2,1,0:T(8,128)S(1)}, s32[]{:S(2)}) %slice-start) | async-done | bytes 917528 | tf_op jit(solution)/shard_map/slice | solution.py:139
  24.3 2.4 %convolution_bitcast_fusion = f32[8,128,2,128]{3,1,2,0:T(8,128)} fusion(f32[7,2,128,128]{3,2,1,0:T(8,128)S(1)} %slice-done, bf16[8,128,2,128]{3,2,1,0:T(2,128)(2,1)} %reshape_reshape.15, f32[8]{0:T(128)S(1)} %fusion.66), kind=kOutput, calls=%fused_computation.21 | convolution fusion | flops 67633152 | bytes 2490400 | tf_op jit(solution)/shard_map/mthd,mhde->mthe/dot_general | solution.py:145
  32.4 2.4 %copy.92 = f32[8,128,2,128]{3,1,0,2:T(8,128)} copy(f32[8,128,2,128]{3,1,2,0:T(8,128)} %convolution_bitcast_fusion) | data formatting | bytes 2097152 | tf_op jit(solution)/shard_map/mthd,mhde->mthe/transpose | solution.py:145
  34.8 2.5 %copy.97 = f32[4,256,2,128]{3,1,0,2:T(8,128)} copy(f32[4,256,2,128]{1,3,2,0:T(8,128)} %convolution_bitcast_fusion.2) | data formatting | bytes 2097152 | tf_op jit(solution)/shard_map/mthd,mhde->mthe/transpose | solution.py:145
  37.4 1.7 %bitcast_reduce_fusion = f32[2,2,128,128]{3,2,1,0:T(8,128)S(1)} fusion(f32[16,2,128,128]{3,2,1,0:T(8,128)} %get-tuple-element.26), kind=kLoop, calls=%fused_computation.8 | loop fusion | flops 458752 | bytes 2359296 | tf_op jit(solution)/shard_map/reduce_sum | solution.py:136
  40.6 2.6 %copy.102 = f32[2,512,2,128]{3,1,0,2:T(8,128)} copy(f32[2,512,2,128]{1,3,2,0:T(8,128)} %convolution_bitcast_fusion.1) | data formatting | bytes 2097152 | tf_op jit(solution)/shard_map/mthd,mhde->mthe/transpose | solution.py:145
  43.2 3.2 %fusion.16 = f32[16,64,2,128]{3,1,2,0:T(8,128)} fusion(f32[15,2,128,128]{3,2,1,0:T(8,128)} %slice.63, f32[16]{0:T(128)S(1)} %fusion.65, f32[16,64,2]{1,2,0:T(2,128)S(1)} %copy.86, bf16[16,64,2,128]{3,2,1,0:T(2,128)(2,1)} %reshape.263), kind=kOutput, calls=%fused_computation.31 | convolution fusion | flops 68419584 | bytes 3547200 | tf_op jit(solution)/shard_map/mthd,mhde->mthe/dot_general | solution.py:145
  46.5 4.7 %fusion.15 = f32[16,64,2,128]{3,1,2,0:T(8,128)} fusion(f32[16,64,2,128]{3,1,2,0:T(8,128)} %fusion.16, f32[16,64,2,128]{3,1,0,2:T(8,128)} %bitcast.109, f32[16,64,2,128]{3,1,0,2:T(8,128)} %bitcast.108, f32[16,64,2,128]{3,1,0,2:T(8,128)} %bitcast.107, f32[16,64,2]{1,2,0:T(2,128)S(1)} %copy.99, f32[16,64,2]{1,2,0:T(2,128)S(1)} %copy.94, ...), kind=kOutput, calls=%fused_computation.29 | convolution fusion | flops 69468160 | bytes 6852608 | tf_op jit(solution)/shard_map/jhts,jshd->jthd/dot_general | solution.py:129
  52.7 3.4 %all-gather.2.cloned.1.call-done = f32[8,256,128]{2,1,0:T(8,128)} async-done(((f32[1,256,128]{2,1,0:T(8,128)}), f32[8,256,128]{2,1,0:T(8,128)}) %all-gather.2.cloned.1.call-update) | async-done | bytes 1048592 | tf_op jit(solution)/shard_map/all_gather | solution.py:104
  56.1 2.4 %convolution_convert_fusion.1 = bf16[3,256,128]{2,0,1:T(4,128)(2,1)S(1)} fusion(f32[8,256,128]{2,1,0:T(8,128)} %all-gather.2.cloned.1.call-done, s32[3]{0:T(128)S(1)} %get-tuple-element.29, s32[3]{0:T(128)S(1)} %get-tuple-element.30), kind=kOutput, calls=%fused_computation.38 | convolution fusion | flops 9535560 | bytes 1245208 | tf_op jit(solution)/shard_map/nb,nxy->bxy/dot_general | solution.py:113
  58.5 2.7 %fusion.1 = f32[1024,2,128]{0,2,1:T(8,128)} fusion(f32[1024,2,3]{0,2,1:T(4,128)S(1)} %slice_multiply_fusion, bf16[1024,2,128,1]{2,1,0,3:T(2,128)(2,1)} %bitcast.114, bf16[3,2,128,128]{3,0,2,1:T(4,128)(2,1)S(1)} %bitcast.117), kind=kOutput, calls=%fused_computation.6 | convolution fusion | flops 202637312 | bytes 1794048 | tf_op jit(solution)/shard_map/thd,bhde->tbhe/dot_general | solution.py:154
  61.2 2.6 %copy.123 = f32[1024,2,128]{2,0,1:T(8,128)} copy(f32[1024,2,128]{0,2,1:T(8,128)} %fusion.1) | data formatting | bytes 2097152 | tf_op jit(solution)/shard_map/tbhe,thb->the/dot_general | solution.py:164
  67.9 11.4 %all_to_all.30 = bf16[4,256,256]{2,1,0:T(8,128)(2,1)S(1)} all-to-all(bf16[4,256,256]{2,1,0:T(8,128)(2,1)S(1)} %reshape.274), channel_id=1, replica_groups=mesh['ctx'=8,'head'=4] {'head'}, dimensions={0} | all-to-all | bytes 1048576 | tf_op jit(solution)/shard_map/all_to_all | solution.py:176
  79.5 1.9 %fusion.20 = (f32[256]{0:T(256)S(1)}, bf16[256,1024]{1,0:T(8,128)(2,1)S(1)}) fusion(bf16[256,1024]{0,1:T(8,128)(2,1)S(1)} %bitcast.112, bf16[1024,1024]{1,0:T(8,128)(2,1)S(1)} %copy-done, bf16[256,1024]{1,0:T(8,128)(2,1)} %param.18), kind=kOutput, calls=%fused_computation.39 | convolution fusion | flops 538443520 | bytes 3671040 | tf_op jit(solution)/shard_map/grc,cd->grd/dot_general | solution.py:174
  81.4 4.9 %fusion.10 = bf16[32,8,24,128]{3,1,2,0:T(8,128)(2,1)S(1)} fusion(bf16[1024,3072]{1,0:T(8,128)(2,1)} %param.21, bf16[256,1024]{1,0:T(8,128)(2,1)S(1)} %get-tuple-element.28, f32[1024]{0:T(1024)S(1)} %copy-done.18, f32[256]{0:T(256)S(1)} %add_rsqrt_fusion.1), kind=kOutput, calls=%fused_computation.19 | convolution fusion | flops 1612447744 | bytes 8393728 | tf_op jit(solution)/shard_map/dot_general | solution.py:185
  89.2 2.4 %collective-permute-start = (bf16[256,2,8,128]{3,0,2,1:T(8,128)(2,1)}, bf16[256,2,8,128]{3,0,2,1:T(8,128)(2,1)}, u32[]{:S(2)}, u32[]{:S(2)}) collective-permute-start(bf16[256,2,8,128]{3,0,2,1:T(8,128)(2,1)} %copy.127), channel_id=1, source_target_pairs={{0,1},{1,2},{2,3},{3,4},{4,5},{5,6},{6,7},{7,8},{8,9},{9,10},{10,1... | collective-permute-start | bytes 3145736 | tf_op jit(solution)/shard_map/ppermute | solution.py:17
  96.9 2.6 %fusion.23 = f32[8,256,512]{2,1,0:T(8,128)} fusion(bf16[512,2,8,128]{3,0,2,1:T(8,128)(2,1)S(1)} %constant_dynamic-update-slice_fusion, bf16[256,1,8,128]{3,2,1,0:T(8,128)(2,1)S(1)} %slice.73), kind=kOutput, calls=%fused_computation.43 | convolution fusion | flops 268435456 | bytes 5767168 | tf_op jit(solution)/shard_map/while/body/eval_jaxpr/qhd,khd->hqk/dot_general | solution.py:28
  99.6 3.3 %fusion.82 = f32[8,256]{1,0:T(8,128)S(1)} fusion(s32[256,512]{1,0:T(8,128)S(1)} %copy-done.11, s32[8]{0:T(128)S(1)} %copy-done.19, pred[512]{0:T(512)(128)(4,1)S(1)} %broadcast_compare_fusion.1, pred[256,512]{1,0:T(8,128)(4,1)S(1)} %broadcast_compare_fusion, bf16[512,2,8,128]{3,0,2,1:T(8,128)(2,1)} %copy-done.9, bf16[256,1,8,128]{3,2,1,0:T(8,128)(2,1)} %copy-done.10), kind=kOutput, calls=%fused_computation.140 | convolution fusion | flops 275776000 | bytes 2236960 | tf_op jit(solution)/shard_map/while/body/eval_jaxpr/sub | solution.py:39
  102.9 6.0 %fusion.19 = bf16[8,128,256]{2,1,0:T(8,128)(2,1)S(1)} fusion(f32[8,256]{1,0:T(8,128)S(1)} %fusion.82, bf16[512,2,8,128]{3,0,2,1:T(8,128)(2,1)} %copy-done.9, f32[8,256,512]{2,1,0:T(8,128)} %fusion.23, s32[256,512]{1,0:T(8,128)S(1)} %copy-done.11, s32[8]{0:T(128)S(1)} %copy-done.19, pred[512]{0:T(512)(128)(4,1)S(1)} %broadcast_compare_fusion.1, ...), kind=kOutput, calls=%fused_computation.37 | convolution fusion | flops 277088768 | bytes 6431264 | tf_op jit(solution)/shard_map/while/body/eval_jaxpr/hqk,khd->qhd/dot_general | solution.py:42
  109.0 22.0 %all_to_all.31 = bf16[256,4,256]{0,2,1:T(8,128)(2,1)S(1)} all-to-all(bf16[256,4,256]{0,2,1:T(8,128)(2,1)S(1)} %bitcast.116), channel_id=1, replica_groups=mesh['ctx'=8,'head'=4] {'head'}, dimensions={1} | all-to-all | bytes 1048576 | tf_op jit(solution)/shard_map/all_to_all | solution.py:199
  (91 shorter events, 28.3 us)
Async XLA Ops:
  7.2 72.3 %copy-start = (bf16[1024,1024]{1,0:T(8,128)(2,1)S(1)}, bf16[1024,1024]{1,0:T(8,128)(2,1)}, u32[]{:S(2)}) copy-start(bf16[1024,1024]{1,0:T(8,128)(2,1)} %param.19) | copy-start | bytes 6291460
  7.2 48.9 %all-gather.2.cloned.1.call-start = ((), (), s32[]{:S(2)}) async-start(), calls=%async_computation.2 | async-start | bytes 1179648 | tf_op jit(solution)/shard_map/all_gather | solution.py:104
  9.7 0.9 copy-start.5
  13.1 3.9 %copy-start.3 = (bf16[1024,256]{1,0:T(8,128)(2,1)S(1)}, bf16[1024,256]{1,0:T(8,128)(2,1)}, u32[]{:S(2)}) copy-start(bf16[1024,256]{1,0:T(8,128)(2,1)} %param.12) | copy-start | bytes 1572868
  13.1 3.0 %copy-start.1 = (f32[16,2,128,128]{3,2,1,0:T(8,128)S(1)}, f32[16,2,128,128]{3,2,1,0:T(8,128)}, u32[]{:S(2)}) copy-start(f32[16,2,128,128]{3,2,1,0:T(8,128)} %get-tuple-element.26) | copy-start | bytes 6291460
  16.1 2.7 %copy-start.17 = (f32[16,2,8]{0,2,1:T(8,128)S(1)}, f32[16,2,8]{0,2,1:T(8,128)}, u32[]{:S(2)}) copy-start(f32[16,2,8]{0,2,1:T(8,128)} %param.16) | copy-start | bytes 3076
  17.9 8.8 %slice-start.1 = ((f32[4,2,128,128]{3,2,1,0:T(8,128)}), f32[3,2,128,128]{3,2,1,0:T(8,128)S(1)}, s32[]{:S(2)}) async-start(f32[4,2,128,128]{3,2,1,0:T(8,128)} %bitcast_reduce_fusion.1), calls=%async_computation.4 | async-start | bytes 786432 | tf_op jit(solution)/shard_map/slice | solution.py:139
  22.2 2.1 %slice-start = ((f32[8,2,128,128]{3,2,1,0:T(8,128)}), f32[7,2,128,128]{3,2,1,0:T(8,128)S(1)}, s32[]{:S(2)}) async-start(f32[8,2,128,128]{3,2,1,0:T(8,128)} %bitcast_reduce_fusion.2), calls=%async_computation.3 | async-start | bytes 1835008 | tf_op jit(solution)/shard_map/slice | solution.py:139
  22.2 4.5 %copy-start.7 = (bf16[4,256,2,128]{3,2,1,0:T(2,128)(2,1)S(1)}, bf16[4,256,2,128]{3,2,1,0:T(2,128)(2,1)}, u32[]{:S(2)}) copy-start(bf16[4,256,2,128]{3,2,1,0:T(2,128)(2,1)} %reshape_reshape.16) | copy-start | bytes 1572868
  22.2 5.9 %copy-start.13 = (f32[16,64,2,8]{1,0,3,2:T(8,128)S(1)}, f32[16,64,2,8]{1,0,3,2:T(8,128)}, u32[]{:S(2)}) copy-start(f32[16,64,2,8]{1,0,3,2:T(8,128)} %reshape.262) | copy-start | bytes 196612
  22.2 5.9 %copy-start.2 = (f32[16,2,128,128]{3,2,1,0:T(8,128)S(1)}, f32[16,2,128,128]{3,2,1,0:T(8,128)}, u32[]{:S(2)}) copy-start(f32[16,2,128,128]{3,2,1,0:T(8,128)} %get-tuple-element.26) | copy-start | bytes 6291460
  32.4 6.7 %copy-start.8 = (bf16[2,512,2,128]{3,2,1,0:T(2,128)(2,1)S(1)}, bf16[2,512,2,128]{3,2,1,0:T(2,128)(2,1)}, u32[]{:S(2)}) copy-start(bf16[2,512,2,128]{3,2,1,0:T(2,128)(2,1)} %reshape_reshape.17) | copy-start | bytes 1572868
  40.6 5.9 %copy-start.6 = (bf16[16,64,2,128]{3,2,1,0:T(2,128)(2,1)S(1)}, bf16[16,64,2,128]{3,2,1,0:T(2,128)(2,1)}, u32[]{:S(2)}) copy-start(bf16[16,64,2,128]{3,2,1,0:T(2,128)(2,1)} %copy-done.5) | copy-start | bytes 1572868
  46.5 6.1 %copy-start.14 = (f32[1024,16]{0,1:T(8,128)S(1)}, f32[1024,16]{0,1:T(8,128)}, u32[]{:S(2)}) copy-start(f32[1024,16]{0,1:T(8,128)} %fusion.35) | copy-start | bytes 196612
  46.5 6.1 %copy-start.16 = (f32[3]{0:T(128)S(1)}, f32[3]{0:T(128)}, u32[]{:S(2)}) copy-start(f32[3]{0:T(128)} %constant.134.clone) | copy-start | bytes 40
  58.5 6.9 %copy-start.15 = (f32[256]{0:T(256)S(1)}, f32[256]{0:T(256)}, u32[]{:S(2)}) copy-start(f32[256]{0:T(256)} %param.17) | copy-start | bytes 3076
  67.9 13.5 %copy-start.18 = (f32[1024]{0:T(1024)S(1)}, f32[1024]{0:T(1024)}, u32[]{:S(2)}) copy-start(f32[1024]{0:T(1024)} %param.20) | copy-start | bytes 12292
  81.4 4.9 %copy-start.12 = (bf16[256,1024]{1,0:T(8,128)(2,1)}, bf16[256,1024]{1,0:T(8,128)(2,1)S(1)}, u32[]{:S(2)}) copy-start(bf16[256,1024]{1,0:T(8,128)(2,1)S(1)} %get-tuple-element.28) | copy-start | bytes 1572868
  86.6 1.2 copy-start.4
  89.2 4.5 %collective-permute-start = (bf16[256,2,8,128]{3,0,2,1:T(8,128)(2,1)}, bf16[256,2,8,128]{3,0,2,1:T(8,128)(2,1)}, u32[]{:S(2)}, u32[]{:S(2)}) collective-permute-start(bf16[256,2,8,128]{3,0,2,1:T(8,128)(2,1)} %copy.127), channel_id=1, source_target_pairs={{0,1},{1,2},{2,3},{3,4},{4,5},{5,6},{6,7},{7,8},{8,9},{9,10},{10,1... | collective-permute-start | bytes 3145736 | tf_op jit(solution)/shard_map/ppermute | solution.py:17
  93.7 1.9 %copy-start.10 = (bf16[256,1,8,128]{3,2,1,0:T(8,128)(2,1)}, bf16[256,1,8,128]{3,2,1,0:T(8,128)(2,1)S(1)}, u32[]{:S(2)}) copy-start(bf16[256,1,8,128]{3,2,1,0:T(8,128)(2,1)S(1)} %slice.73) | copy-start | bytes 1572868
  95.6 1.3 copy-start.9
  96.9 2.6 %copy-start.11 = (s32[256,512]{1,0:T(8,128)S(1)}, s32[256,512]{1,0:T(8,128)}, u32[]{:S(2)}) copy-start(s32[256,512]{1,0:T(8,128)} %broadcast_subtract_fusion) | copy-start | bytes 1572868
  96.9 2.6 %copy-start.19 = (s32[8]{0:T(128)S(1)}, s32[8]{0:T(128)}, u32[]{:S(2)}) copy-start(s32[8]{0:T(128)} %param.22) | copy-start | bytes 100
Sparse Core Ops, SparseCore 0:
  13.2 42.8 all-gather.1
where the time goes:
time: 140 us; the launch traced here: 139 us
  matrix products  41.3 us (30%)
  local copies, waits for them, and re-layouts  33.8 us (24%)
  blocking collectives  33.4 us (24%)
  between operations  14.4 us (10%)
  other arithmetic  10.1 us (7%)
  waiting for transfers between devices  3.41 us (2%)
  starting transfers between devices  2.41 us (2%)
    all_to_all x1, blocking collectives, per_device(): lax.all_to_all(spread, 'head', split_axis=1, concat_axis=0, tiled=True)  22 us
    all_to_all x1, blocking collectives, per_device(): lax.all_to_all(sectioned, 'head', split_axis=0, concat_axis=2, tiled=True)  11.4 us
    dot_general x4, matrix products, per_device(): jnp.einsum('mthd,mhde->mthe', blocked_query, read_state, preferred_elemen...  8.49 us
    transpose x3, local copies, waits for them, and re-layouts, per_device(): jnp.einsum('mthd,mhde->mthe', blocked_query, read_state, preferred_elemen...  7.52 us
    unnamed x43, local copies, waits for them, and re-layouts  6.44 us
    dot_general x1, matrix products, attend_block(): jnp.einsum('hqk,khd->qhd', probs, value_block, preferred_element_type=jnp...  6.04 us
    reduce_sum x3, other arithmetic, per_device(): jnp.sum(states.reshape(group_total, block_len, local_heads, head_dim, hea...  5.61 us
    dot_general x1, matrix products, per_device(): jnp.dot(normed, w_qkv, preferred_element_type=jnp.float32)  4.86 us
  transfers between devices with their start and end apart: 2, of which 1 were waited for; matrix products, arithmetic and copies ran while one was open for 28% of the time, Pallas kernels for 0%

commit v1 on v0

v1 whole, which is shorter than its diff:
```python
import functools
import math

import jax
import jax.numpy as jnp
from jax import lax
from jax.experimental import pallas as pl
from jax.experimental.pallas import tpu as pltpu
from jax.sharding import PartitionSpec as P

STRETCH = 64
EPSILON = 1e-05
MESH = pl.DeviceIdType.MESH
F32 = jnp.float32
BF16 = jnp.bfloat16


def dot(a, b):
    return jnp.dot(a, b, preferred_element_type=F32)


def dot_tn(a, b):
    return lax.dot_general(a, b, (((0,), (0,)), ((), ())), preferred_element_type=F32)


def dot_nt(a, b):
    return lax.dot_general(a, b, (((1,), (1,)), ((), ())), preferred_element_type=F32)


def kernel(
    n_ctx,
    group,
    local_heads,
    q_hbm,
    k_hbm,
    v_hbm,
    index_ref,
    table_ref,
    head_gain_ref,
    res_hbm,
    w_out_hbm,
    norm_gain_ref,
    w_qkv_hbm,
    windows_ref,
    hidden_ref,
    attended_ref,
    q_ref,
    k_ref,
    v_ref,
    res_ref,
    ho_ref,
    w_out_ref,
    w_qkv_ref,
    acc_ref,
    read_ref,
    cur_ref,
    state_send,
    state_recv,
    spread_ref,
    qs_ref,
    kv_ref,
    local_sem,
    st_send_sem,
    st_recv_sem,
    res_send_sem,
    res_recv_sem,
    ho_send_sem,
    ho_recv_sem,
    halo_send_sem,
    halo_recv_sem,
):
    tokens, width = q_ref.shape
    dim = width // local_heads
    rows = tokens // group
    model = w_out_ref.shape[1]
    ctx_bits = n_ctx.bit_length() - 1
    chunk_bits = group.bit_length() - 1
    inner = rows // STRETCH
    inner_bits = inner.bit_length() - 1
    levels = 1 + inner_bits + chunk_bits + ctx_bits
    ntab = table_ref.shape[0]
    hops = group // 2 - 1

    pos = lax.axis_index("ctx")
    me = lax.axis_index("head")
    sib = me + 1 - 2 * lax.rem(me, 2)

    def ahead(j):
        return lax.rem(me + 2 * j, group)

    def behind(j):
        return lax.rem(me + group - 2 * j, group)

    def bit_of(b):
        return lax.rem(pos // (2**b), 2)

    def partner(b):
        return pos + 2**b - 2 ** (b + 1) * bit_of(b)

    loads = []

    def load(src, dst):
        copy = pltpu.make_async_copy(src, dst, local_sem.at[len(loads)])
        copy.start()
        loads.append(copy)
        return copy

    load_k = load(k_hbm, k_ref)
    load_v = load(v_hbm, v_ref)
    load_q = load(q_hbm, q_ref)
    load_res = load(res_hbm, res_ref.at[me])
    load_wo = load(w_out_hbm, w_out_ref)
    load_w3 = [
        load(
            w_qkv_hbm.at[:, pl.ds(pl.multiple_of(s * model + me * width, width), width)],
            w_qkv_ref.at[:, pl.ds(s * width, width)],
        )
        for s in range(3)
    ]

    barrier = pltpu.get_barrier_semaphore()
    pl.semaphore_signal(barrier, inc=1, device_id={"head": sib}, device_id_type=MESH)
    for j in range(1, hops + 1):
        pl.semaphore_signal(barrier, inc=1, device_id={"head": ahead(j)}, device_id_type=MESH)
    for b in range(ctx_bits):
        pl.semaphore_signal(barrier, inc=1, device_id={"ctx": partner(b)}, device_id_type=MESH)

    @pl.when(pos > 0)
    def _():
        pl.semaphore_signal(barrier, inc=1, device_id={"ctx": pos - 1}, device_id_type=MESH)

    @pl.when(pos < n_ctx - 1)
    def _():
        pl.semaphore_signal(barrier, inc=1, device_id={"ctx": pos + 1}, device_id_type=MESH)

    neighbours = jnp.minimum(pos, 1) + jnp.minimum(n_ctx - 1 - pos, 1)
    pl.semaphore_wait(barrier, 1 + hops + ctx_bits + neighbours)

    def remote(src, dst, send, recv, where):
        return pltpu.make_async_remote_copy(
            src_ref=src,
            dst_ref=dst,
            send_sem=send,
            recv_sem=recv,
            device_id=where,
            device_id_type=MESH,
        )

    def res_copy(slot, source, to):
        src = res_hbm if slot <= hops else res_ref.at[source]
        return remote(
            src, res_ref.at[source], res_send_sem.at[slot], res_recv_sem.at[slot], {"head": to}
        )

    def ho_copy(slot, c, source, to):
        block = ho_ref.at[source, c]
        return remote(
            block, block, ho_send_sem.at[slot, c], ho_recv_sem.at[slot, c], {"head": to}
        )

    def state_copy(b):
        return remote(
            state_send.at[b],
            state_recv.at[b],
            st_send_sem.at[b],
            st_recv_sem.at[b],
            {"ctx": partner(b)},
        )

    def halo_copy():
        return remote(
            kv_ref.at[group],
            kv_ref.at[0],
            halo_send_sem,
            halo_recv_sem,
            {"ctx": jnp.minimum(pos + 1, n_ctx - 1)},
        )

    def state_start(b):
        state_send[b] = cur_ref[...].astype(BF16)
        state_copy(b).start()

    def state_finish(b):
        state_copy(b).wait_recv()
        arrived = state_recv[b]
        used = jnp.where(bit_of(b) == 1, arrived, jnp.zeros_like(arrived))
        for h in range(local_heads):
            read_ref[h, :, b * dim : (b + 1) * dim] = used[h * dim : (h + 1) * dim]
        cur_ref[...] += arrived.astype(F32)

    load_k.wait()
    load_v.wait()
    states = []
    for h in range(local_heads):
        cols = slice(h * dim, (h + 1) * dim)
        mine = [
            dot_tn(k_ref[c * rows : (c + 1) * rows, cols], v_ref[c * rows : (c + 1) * rows, cols])
            for c in range(group)
        ]
        states.append(mine)
        cur_ref[cols, :] = functools.reduce(lambda a, b: a + b, mine)
    state_start(0)
    res_copy(0, me, sib).start()
    for j in range(1, hops + 1):
        res_copy(j, me, ahead(j)).start()

    for h in range(local_heads):
        for level in range(levels):
            column = h * levels + level
            rate = (STRETCH * 2 ** max(level - 1, 0)) ** (-0.5)
            full = jnp.broadcast_to(table_ref[:, column : column + 1] * rate, (ntab, dim))
            high = full.astype(BF16)
            rest = full - high.astype(F32)
            mid = rest.astype(BF16)
            low = (rest - mid.astype(F32)).astype(BF16)
            spread_ref[:, column * dim : (column + 1) * dim] = jnp.concatenate([high, mid, low], 0)

    entry = lax.broadcasted_iota(jnp.int32, (3 * ntab, rows), 0)
    entry = lax.rem(entry, ntab)

    def weights(offset, h, first, count):
        chosen = jnp.broadcast_to(index_ref[:, pl.ds(offset, rows)], (3 * ntab, rows))
        onehot = (chosen == entry).astype(F32).astype(BF16)
        start = (h * levels + first) * dim
        return dot_tn(onehot, spread_ref[:, start : start + count * dim])

    t = lax.broadcasted_iota(jnp.int32, (rows, rows), 0)
    s = lax.broadcasted_iota(jnp.int32, (rows, rows), 1)
    load_q.wait()

    def near(c):
        offset = c * rows
        span = slice(offset, offset + rows)
        tc = t // STRETCH
        sc = s // STRETCH
        for h in range(local_heads):
            cols = slice(h * dim, (h + 1) * dim)
            w = weights(offset, h, 0, 1 + inner_bits + chunk_bits)

            def wide(level):
                return jnp.concatenate([w[:, level * dim : (level + 1) * dim]] * (rows // dim), 1)

            q = q_ref[span, cols]
            scores = dot_nt(q, k_ref[span, cols])
            factor = jnp.where((tc == sc) & (s <= t), wide(0), 0.0)
            for b in range(inner_bits):
                member = (sc // 2**b) == (tc // 2**b) - 1
                member &= lax.rem(tc // 2**b, 2) == 1
                factor = jnp.where(member, wide(1 + b), factor)
            out = dot((scores * factor).astype(BF16), v_ref[span, cols])
            for b in range(chunk_bits):
                first = (c >> (b + 1)) << (b + 1)
                last = (c >> b) << b
                if last > first:
                    bucket = functools.reduce(lambda x, y: x + y, states[h][first:last])
                    level = 1 + inner_bits + b
                    out += w[:, level * dim : (level + 1) * dim] * dot(q, bucket.astype(BF16))
            acc_ref[span, cols] = out

    for i in range(group):
        near(group - 1 - i)
        if i < ctx_bits - 1:
            state_finish(i)
            state_start(i + 1)
    for b in range(min(group, ctx_bits - 1), ctx_bits):
        state_finish(b)
        if b < ctx_bits - 1:
            state_start(b + 1)

    def far(i, carry):
        c = group - 1 - i
        offset = pl.multiple_of(c * rows, rows)
        span = pl.ds(offset, rows)
        for h in range(local_heads):
            cols = slice(h * dim, (h + 1) * dim)
            w = weights(offset, h, 1 + inner_bits + chunk_bits, ctx_bits)
            part = w * dot(q_ref[span, cols], read_ref[h])
            out = acc_ref[span, cols]
            for b in range(ctx_bits):
                out += part[:, b * dim : (b + 1) * dim]
            square = jnp.mean(out * out, -1, keepdims=True)
            out = out * lax.rsqrt(square + EPSILON) * head_gain_ref[:, cols]
            ho_ref[me, c, :, cols] = out.astype(BF16)
        for j in range(1, hops + 1):
            ho_copy(j, c, me, ahead(j)).start()
        ho_copy(0, c, me, sib).start()
        return carry

    lax.fori_loop(0, group, far, 0)

    load_res.wait()
    for j in range(1, hops + 1):
        res_copy(j, behind(j), me).wait_recv()
        res_copy(hops + j, behind(j), sib).start()
    load_wo.wait()
    for copy in load_w3:
        copy.wait()

    def forward(c):
        for j in range(1, hops + 1):
            ho_copy(j, c, behind(j), me).wait_recv()
            ho_copy(hops + j, c, behind(j), sib).start()

    def forwarded(j):
        return lax.rem(sib + group - 2 * j, group)

    forward(group - 1)
    res_copy(0, sib, me).wait_recv()
    for j in range(1, hops + 1):
        res_copy(hops + j, forwarded(j), me).wait_recv()

    score_scale = dim ** (-0.5) * math.log2(math.e)

    def attend(c, first):
        offset = c * rows
        if not isinstance(c, int):
            offset = pl.multiple_of(offset, rows)
        for h in range(local_heads):
            cols = slice(h * dim, (h + 1) * dim)
            window = windows_ref[me * local_heads + h]
            before = jnp.where(pos == 0, 0, window) if first else window
            q = qs_ref[c, :, cols]
            distance = t - s
            old = dot_nt(q, kv_ref[c, 0, :, cols]) * score_scale
            new = dot_nt(q, kv_ref[c + 1, 0, :, cols]) * score_scale
            old = jnp.where(distance + rows < before, old, -1e30)
            new = jnp.where((distance >= 0) & (distance < window), new, -1e30)
            top = jnp.max(jnp.maximum(old, new), -1, keepdims=True)
            old = jnp.exp2(old - top)
            new = jnp.exp2(new - top)
            total = jnp.sum(old + new, -1, keepdims=True)
            out = dot(old.astype(BF16), kv_ref[c, 1, :, cols])
            out += dot(new.astype(BF16), kv_ref[c + 1, 1, :, cols])
            attended_ref[pl.ds(offset, rows), cols] = (out * (1.0 / total)).astype(BF16)

    def project(i, carry):
        c = group - 1 - i
        ho_copy(0, c, sib, me).wait_recv()
        for j in range(1, hops + 1):
            ho_copy(hops + j, c, forwarded(j), me).wait_recv()
        heads = jnp.concatenate([ho_ref[g, c] for g in range(group)], 1)
        hidden = (res_ref[c].astype(F32) + dot(heads, w_out_ref[...])).astype(BF16)

        @pl.when(c == me)
        def _():
            hidden_ref[...] = hidden

        hidden = hidden.astype(F32)
        square = jnp.mean(hidden * hidden, -1, keepdims=True)
        normed = (hidden * lax.rsqrt(square + EPSILON) * norm_gain_ref[...]).astype(BF16)
        qkv = dot(normed, w_qkv_ref[...]).astype(BF16)
        qs_ref[c] = qkv[:, :width]
        kv_ref[c + 1, 0] = qkv[:, width : 2 * width]
        kv_ref[c + 1, 1] = qkv[:, 2 * width :]

        @pl.when((i == 0) & (pos < n_ctx - 1))
        def _():
            halo_copy().start()

        @pl.when(i < group - 1)
        def _():
            forward(c - 1)

        @pl.when(i > 0)
        def _():
            attend(c + 1, False)

        return carry

    lax.fori_loop(0, group, project, 0)

    @pl.when(pos > 0)
    def _():
        halo_copy().wait_recv()

    @pl.when(pos == 0)
    def _():
        kv_ref[0] = jnp.zeros(kv_ref.shape[1:], BF16)

    attend(0, True)

    @pl.when(pos < n_ctx - 1)
    def _():
        halo_copy().wait_send()

    for b in range(ctx_bits):
        state_copy(b).wait_send()
    res_copy(0, me, sib).wait_send()
    for j in range(1, hops + 1):
        res_copy(j, me, ahead(j)).wait_send()
        res_copy(hops + j, behind(j), sib).wait_send()
    for c in range(group):
        ho_copy(0, c, me, sib).wait_send()
        for j in range(1, hops + 1):
            ho_copy(j, c, me, ahead(j)).wait_send()
            ho_copy(hops + j, c, behind(j), sib).wait_send()


def per_device(
    n_ctx,
    group,
    queries,
    keys,
    values,
    level_index,
    level_table,
    head_gain,
    residual,
    w_out,
    norm_gain,
    w_qkv,
    windows,
):
    tokens, width = queries.shape
    ntab, local_heads, levels = level_table.shape
    dim = width // local_heads
    rows = tokens // group
    model = w_out.shape[1]
    ctx_bits = n_ctx.bit_length() - 1
    slots = 1 + 2 * (group // 2 - 1)
    vmem = pl.BlockSpec(memory_space=pltpu.VMEM)
    smem = pl.BlockSpec(memory_space=pltpu.SMEM)
    anywhere = pl.BlockSpec(memory_space=pl.ANY)
    dma = pltpu.SemaphoreType.DMA
    call = pl.pallas_call(
        functools.partial(kernel, n_ctx, group, local_heads),
        out_shape=(
            jax.ShapeDtypeStruct(residual.shape, BF16),
            jax.ShapeDtypeStruct(queries.shape, BF16),
        ),
        in_specs=[
            anywhere,
            anywhere,
            anywhere,
            vmem,
            vmem,
            vmem,
            anywhere,
            anywhere,
            vmem,
            anywhere,
            smem,
        ],
        out_specs=(vmem, vmem),
        scratch_shapes=[
            pltpu.VMEM((tokens, width), BF16),
            pltpu.VMEM((tokens, width), BF16),
            pltpu.VMEM((tokens, width), BF16),
            pltpu.VMEM((group, rows, model), BF16),
            pltpu.VMEM((group, group, rows, width), BF16),
            pltpu.VMEM(w_out.shape, BF16),
            pltpu.VMEM((model, 3 * width), BF16),
            pltpu.VMEM((tokens, width), F32),
            pltpu.VMEM((local_heads, dim, ctx_bits * dim), BF16),
            pltpu.VMEM((width, dim), F32),
            pltpu.VMEM((ctx_bits, width, dim), BF16),
            pltpu.VMEM((ctx_bits, width, dim), BF16),
            pltpu.VMEM((3 * ntab, local_heads * levels * dim), BF16),
            pltpu.VMEM((group, rows, width), BF16),
            pltpu.VMEM((group + 1, 2, rows, width), BF16),
            dma((8,)),
            dma((ctx_bits,)),
            dma((ctx_bits,)),
            dma((slots,)),
            dma((slots,)),
            dma((slots, group)),
            dma((slots, group)),
            dma,
            dma,
        ],
        compiler_params=pltpu.CompilerParams(
            collective_id=0, has_side_effects=True, vmem_limit_bytes=48 * 2**20
        ),
    )
    return call(
        queries,
        keys,
        values,
        level_index.reshape(1, tokens),
        level_table.reshape(ntab, local_heads * levels),
        head_gain.reshape(1, width),
        residual,
        w_out,
        norm_gain.reshape(1, model),
        w_qkv,
        windows,
    )


def solution(mesh):
    in_specs = (
        P("ctx", "head"),
        P("ctx", "head"),
        P("ctx", "head"),
        P("ctx"),
        P(None, "head", None),
        P("head"),
        P(("ctx", "head"), None),
        P(),
        P(),
        P(),
        P(),
    )
    out_specs = (P(("ctx", "head"), None), P("ctx", "head"))
    return jax.shard_map(
        functools.partial(per_device, mesh.shape["ctx"], mesh.shape["head"]),
        mesh=mesh,
        in_specs=in_specs,
        out_specs=out_specs,
        check_vma=False,
    )
```

time: 140 us -> 47.6 us (0.34)
  matrix products: 41.3 us -> 0 us
  Pallas kernels: 0 us -> 35.6 us
  blocking collectives: 33.4 us -> 0 us
  local copies, waits for them, and re-layouts: 33.8 us -> 10.8 us
  between operations: 14.4 us -> 0.65 us
  other arithmetic: 10.1 us -> 0 us
  waiting for transfers between devices: 3.41 us -> 0 us
  starting transfers between devices: 2.41 us -> 0 us
    dot_general x13 -> x0, matrix products: 38 us -> none  [the longest x4 8.49 us: per_device(): jnp.einsum('mthd,mhde->mthe', blocked_query, read_state, preferred_elemen...]
    pallas_call x0 -> x1, Pallas kernels: none -> 35.6 us  [per_device(): call(queries, keys, values, level_index.reshape(1, tokens), level_table.r...]
    all_to_all x2 -> x0, blocking collectives: 33.4 us -> none  [the longest x1 22 us: per_device(): lax.all_to_all(spread, 'head', split_axis=1, concat_axis=0, tiled=True)]
    transpose x3 -> x0, local copies, waits for them, and re-layouts: 7.52 us -> none  [per_device(): jnp.einsum('mthd,mhde->mthe', blocked_query, read_state, preferred_elemen...]
    reduce_sum x4 -> x0, other arithmetic: 7.19 us -> none  [the longest x3 5.61 us: per_device(): jnp.sum(states.reshape(group_total, block_len, local_heads, head_dim, hea...]
    reshape x6 -> x1, local copies, waits for them, and re-layouts: 6.22 us -> 0.77 us  [per_device(): level_table.reshape(ntab, local_heads * levels)]
    slice x8 -> x0, local copies, waits for them, and re-layouts: 4.81 us -> none  [the longest x6 3.56 us: per_device(): earlier = jnp.concatenate([jnp.zeros_like(grouped[:1]), grouped[:-1]], 0)]
    unnamed x43 -> x20, local copies, waits for them, and re-layouts: 6.44 us -> 10.1 us
  transfers between devices with their start and end apart: 2 -> 0, of which waited for: 1 -> 0; matrix products, arithmetic and copies ran while one was open for 28% -> 0% of each run, Pallas kernels for 0% -> 0%
where the time goes in v1:
time: 47.6 us; the launch traced here: 47.1 us
  Pallas kernels  35.6 us (75%)
  local copies, waits for them, and re-layouts  10.8 us (23%)
  between operations  0.65 us (1%)
    pallas_call x1, Pallas kernels, per_device(): call(queries, keys, values, level_index.reshape(1, tokens), level_table.r...  35.6 us
    unnamed x20, local copies, waits for them, and re-layouts  10.1 us

profile of v1, /device:TPU:0, one launch (start us, length us, event | category | flops | bytes accessed | tf_op | source)
XLA Modules:
  0.0 47.1 jit_solution(8185237289595966567)
XLA Ops:
  0.6 0.8 %copy.14.table_ref = f32[16,16]{1,0:T(8,128)S(1)} copy(f32[16,16]{0,1:T(8,128)} %bitcast.7) | data formatting | bytes 2048 | tf_op jit(solution)/shard_map/reshape | solution.py:480
  1.4 0.0 copy-start
  1.4 1.6 %copy-done = bf16[1024,1024]{1,0:T(8,128)(2,1)S(1)} copy-done((bf16[1024,1024]{1,0:T(8,128)(2,1)S(1)}, bf16[1024,1024]{1,0:T(8,128)(2,1)}, u32[]{:S(2)}) %copy-start) | copy-done | bytes 2097176
  3.0 0.0 copy-start.1
  3.0 1.0 %copy-done.1 = bf16[1024,256]{1,0:T(8,128)(2,1)S(1)} copy-done((bf16[1024,256]{1,0:T(8,128)(2,1)S(1)}, bf16[1024,256]{1,0:T(8,128)(2,1)}, u32[]{:S(2)}) %copy-start.1) | copy-done | bytes 524312
  4.0 0.0 copy-start.2
  4.0 1.0 %copy-done.2 = bf16[1024,256]{1,0:T(8,128)(2,1)S(1)} copy-done((bf16[1024,256]{1,0:T(8,128)(2,1)S(1)}, bf16[1024,256]{1,0:T(8,128)(2,1)}, u32[]{:S(2)}) %copy-start.2) | copy-done | bytes 524312
  5.1 0.0 copy-start.3
  5.1 1.0 %copy-done.3 = bf16[1024,256]{1,0:T(8,128)(2,1)S(1)} copy-done((bf16[1024,256]{1,0:T(8,128)(2,1)S(1)}, bf16[1024,256]{1,0:T(8,128)(2,1)}, u32[]{:S(2)}) %copy-start.3) | copy-done | bytes 524312
  6.1 0.0 copy-start.4
  6.1 1.0 %copy-done.4 = bf16[256,1024]{1,0:T(8,128)(2,1)S(1)} copy-done((bf16[256,1024]{1,0:T(8,128)(2,1)S(1)}, bf16[256,1024]{1,0:T(8,128)(2,1)}, u32[]{:S(2)}) %copy-start.4) | copy-done | bytes 524312
  7.2 0.0 copy-start.5
  7.2 0.7 %copy-done.5 = s32[1024]{0:T(1024)S(1)} copy-done((s32[1024]{0:T(1024)S(1)}, s32[1024]{0:T(1024)}, u32[]{:S(2)}) %copy-start.5) | copy-done | bytes 4120
  7.8 0.0 copy-start.6
  7.8 0.7 %copy-done.6 = f32[1024]{0:T(1024)S(1)} copy-done((f32[1024]{0:T(1024)S(1)}, f32[1024]{0:T(1024)}, u32[]{:S(2)}) %copy-start.6) | copy-done | bytes 4120
  8.5 0.0 copy-start.7
  8.5 0.7 %copy-done.7 = f32[256]{0:T(256)S(1)} copy-done((f32[256]{0:T(256)S(1)}, f32[256]{0:T(256)}, u32[]{:S(2)}) %copy-start.7) | copy-done | bytes 1048
  9.2 0.0 copy-start.8
  9.2 0.7 %copy-done.8 = s32[8]{0:T(128)S(1)} copy-done((s32[8]{0:T(128)S(1)}, s32[8]{0:T(128)}, u32[]{:S(2)}) %copy-start.8) | copy-done | bytes 56
  9.9 35.6 %shard_map.122 = (bf16[256,1024]{1,0:T(8,128)(2,1)S(1)}, bf16[1024,256]{1,0:T(8,128)(2,1)S(1)}) custom-call(bf16[1024,256]{1,0:T(8,128)(2,1)S(1)} %copy-done.1, bf16[1024,256]{1,0:T(8,128)(2,1)S(1)} %copy-done.2, bf16[1024,256]{1,0:T(8,128)(2,1)S(1)} %copy-done.3, s32[1,1024]{1,0:T(1,128)S(1)} %bitcast.4, f32[16,16]{1,0:T(8,128)S(1)} %copy.14.table_ref, ...), custom_call_target="tpu_custom_call" | custom-call | tf_op jit(solution)/shard_map/pallas_call | solution.py:475
  45.5 0.8 %copy.17 = bf16[256,1024]{1,0:T(8,128)(2,1)} copy(bf16[256,1024]{1,0:T(8,128)(2,1)S(1)} %get-tuple-element.4) | data formatting | bytes 1048576
  46.3 0.8 %copy.18 = bf16[1024,256]{1,0:T(8,128)(2,1)} copy(bf16[1024,256]{1,0:T(8,128)(2,1)S(1)} %get-tuple-element.5) | data formatting | bytes 1048576
Async XLA Ops:
  1.4 1.6 %copy-start = (bf16[1024,1024]{1,0:T(8,128)(2,1)S(1)}, bf16[1024,1024]{1,0:T(8,128)(2,1)}, u32[]{:S(2)}) copy-start(bf16[1024,1024]{1,0:T(8,128)(2,1)} %w_out_hbm.1) | copy-start | bytes 6291460
  3.0 1.0 %copy-start.1 = (bf16[1024,256]{1,0:T(8,128)(2,1)S(1)}, bf16[1024,256]{1,0:T(8,128)(2,1)}, u32[]{:S(2)}) copy-start(bf16[1024,256]{1,0:T(8,128)(2,1)} %q_hbm.1) | copy-start | bytes 1572868
  4.0 1.0 %copy-start.2 = (bf16[1024,256]{1,0:T(8,128)(2,1)S(1)}, bf16[1024,256]{1,0:T(8,128)(2,1)}, u32[]{:S(2)}) copy-start(bf16[1024,256]{1,0:T(8,128)(2,1)} %k_hbm.1) | copy-start | bytes 1572868
  5.1 1.0 %copy-start.3 = (bf16[1024,256]{1,0:T(8,128)(2,1)S(1)}, bf16[1024,256]{1,0:T(8,128)(2,1)}, u32[]{:S(2)}) copy-start(bf16[1024,256]{1,0:T(8,128)(2,1)} %v_hbm.1) | copy-start | bytes 1572868
  6.1 1.0 %copy-start.4 = (bf16[256,1024]{1,0:T(8,128)(2,1)S(1)}, bf16[256,1024]{1,0:T(8,128)(2,1)}, u32[]{:S(2)}) copy-start(bf16[256,1024]{1,0:T(8,128)(2,1)} %res_hbm.1) | copy-start | bytes 1572868
  7.2 0.7 %copy-start.5 = (s32[1024]{0:T(1024)S(1)}, s32[1024]{0:T(1024)}, u32[]{:S(2)}) copy-start(s32[1024]{0:T(1024)} %param.14) | copy-start | bytes 12292
  7.8 0.7 %copy-start.6 = (f32[1024]{0:T(1024)S(1)}, f32[1024]{0:T(1024)}, u32[]{:S(2)}) copy-start(f32[1024]{0:T(1024)} %param.19) | copy-start | bytes 12292
  8.5 0.7 %copy-start.7 = (f32[256]{0:T(256)S(1)}, f32[256]{0:T(256)}, u32[]{:S(2)}) copy-start(f32[256]{0:T(256)} %param.16) | copy-start | bytes 3076
  9.2 0.7 %copy-start.8 = (s32[8]{0:T(128)S(1)}, s32[8]{0:T(128)}, u32[]{:S(2)}) copy-start(s32[8]{0:T(128)} %windows_ref.1) | copy-start | bytes 100

commit v2 on v1

--- a/solution.py
+++ b/solution.py
@@ -10,6 +10,7 @@
 
 STRETCH = 64
 EPSILON = 1e-05
+VMEM_BYTES = 60 * 2**20
 MESH = pl.DeviceIdType.MESH
 F32 = jnp.float32
 BF16 = jnp.bfloat16
@@ -34,14 +35,14 @@
     q_hbm,
     k_hbm,
     v_hbm,
-    index_ref,
-    table_ref,
-    head_gain_ref,
+    index_hbm,
+    table_hbm,
+    head_gain_hbm,
     res_hbm,
     w_out_hbm,
-    norm_gain_ref,
+    norm_gain_hbm,
     w_qkv_hbm,
-    windows_ref,
+    windows_hbm,
     hidden_ref,
     attended_ref,
     q_ref,
@@ -59,6 +60,11 @@
     spread_ref,
     qs_ref,
     kv_ref,
+    index_ref,
+    table_ref,
+    head_gain_ref,
+    norm_gain_ref,
+    windows_ref,
     local_sem,
     st_send_sem,
     st_recv_sem,
@@ -78,7 +84,7 @@
     inner = rows // STRETCH
     inner_bits = inner.bit_length() - 1
     levels = 1 + inner_bits + chunk_bits + ctx_bits
-    ntab = table_ref.shape[0]
+    ntab = table_ref.shape[1]
     hops = group // 2 - 1
 
     pos = lax.axis_index("ctx")
@@ -107,6 +113,13 @@
 
     load_k = load(k_hbm, k_ref)
     load_v = load(v_hbm, v_ref)
+    small = [
+        load(table_hbm, table_ref),
+        load(index_hbm, index_ref),
+        load(head_gain_hbm, head_gain_ref),
+        load(norm_gain_hbm, norm_gain_ref),
+        load(windows_hbm, windows_ref),
+    ]
     load_q = load(q_hbm, q_ref)
     load_res = load(res_hbm, res_ref.at[me])
     load_wo = load(w_out_hbm, w_out_ref)
@@ -204,16 +217,24 @@
     for j in range(1, hops + 1):
         res_copy(j, me, ahead(j)).start()
 
-    for h in range(local_heads):
-        for level in range(levels):
-            column = h * levels + level
-            rate = (STRETCH * 2 ** max(level - 1, 0)) ** (-0.5)
-            full = jnp.broadcast_to(table_ref[:, column : column + 1] * rate, (ntab, dim))
-            high = full.astype(BF16)
-            rest = full - high.astype(F32)
-            mid = rest.astype(BF16)
-            low = (rest - mid.astype(F32)).astype(BF16)
-            spread_ref[:, column * dim : (column + 1) * dim] = jnp.concatenate([high, mid, low], 0)
+    for copy in small:
+        copy.wait()
+    columns = local_heads * levels
+    place = lax.broadcasted_iota(jnp.int32, (columns, 1), 0)
+    level = lax.rem(place, levels)
+    rate = jnp.full((columns, 1), STRETCH ** (-0.5), F32)
+    for b in range(1, levels - 1):
+        rate = jnp.where(level == b + 1, (STRETCH * 2**b) ** (-0.5), rate)
+    full = table_ref[...] * rate
+    high = full.astype(BF16)
+    rest = full - high.astype(F32)
+    mid = rest.astype(BF16)
+    low = (rest - mid.astype(F32)).astype(BF16)
+    row = lax.broadcasted_iota(jnp.int32, (columns, columns * dim), 0)
+    lane = lax.broadcasted_iota(jnp.int32, (columns, columns * dim), 1)
+    spread = (lane // dim == row).astype(F32).astype(BF16)
+    for i, term in enumerate((high, mid, low)):
+        spread_ref[i * ntab : (i + 1) * ntab] = dot_tn(term, spread).astype(BF16)
 
     entry = lax.broadcasted_iota(jnp.int32, (3 * ntab, rows), 0)
     entry = lax.rem(entry, ntab)
@@ -419,7 +440,6 @@
     ctx_bits = n_ctx.bit_length() - 1
     slots = 1 + 2 * (group // 2 - 1)
     vmem = pl.BlockSpec(memory_space=pltpu.VMEM)
-    smem = pl.BlockSpec(memory_space=pltpu.SMEM)
     anywhere = pl.BlockSpec(memory_space=pl.ANY)
     dma = pltpu.SemaphoreType.DMA
     call = pl.pallas_call(
@@ -428,19 +448,7 @@
             jax.ShapeDtypeStruct(residual.shape, BF16),
             jax.ShapeDtypeStruct(queries.shape, BF16),
         ),
-        in_specs=[
-            anywhere,
-            anywhere,
-            anywhere,
-            vmem,
-            vmem,
-            vmem,
-            anywhere,
-            anywhere,
-            vmem,
-            anywhere,
-            smem,
-        ],
+        in_specs=[anywhere] * 11,
         out_specs=(vmem, vmem),
         scratch_shapes=[
             pltpu.VMEM((tokens, width), BF16),
@@ -458,7 +466,12 @@
             pltpu.VMEM((3 * ntab, local_heads * levels * dim), BF16),
             pltpu.VMEM((group, rows, width), BF16),
             pltpu.VMEM((group + 1, 2, rows, width), BF16),
-            dma((8,)),
+            pltpu.VMEM((1, tokens), jnp.int32),
+            pltpu.VMEM((local_heads * levels, ntab), F32),
+            pltpu.VMEM((1, width), F32),
+            pltpu.VMEM((1, model), F32),
+            pltpu.SMEM(windows.shape, jnp.int32),
+            dma((13,)),
             dma((ctx_bits,)),
             dma((ctx_bits,)),
             dma((slots,)),
@@ -469,7 +482,7 @@
             dma,
         ],
         compiler_params=pltpu.CompilerParams(
-            collective_id=0, has_side_effects=True, vmem_limit_bytes=48 * 2**20
+            collective_id=0, has_side_effects=True, vmem_limit_bytes=VMEM_BYTES
         ),
     )
     return call(
@@ -477,7 +490,7 @@
         keys,
         values,
         level_index.reshape(1, tokens),
-        level_table.reshape(ntab, local_heads * levels),
+        level_table.transpose(1, 2, 0).reshape(local_heads * levels, ntab),
         head_gain.reshape(1, width),
         residual,
         w_out,

time: 47.6 us -> 41.4 us (0.87)
  local copies, waits for them, and re-layouts: 10.8 us -> 3.74 us
  Pallas kernels: 35.6 us -> 36.8 us
    unnamed x20 -> x2, local copies, waits for them, and re-layouts: 10.1 us -> 3.74 us
    pallas_call x1, Pallas kernels: 35.6 us -> 36.8 us  [per_device(): call(queries, keys, values, level_index.reshape(1, tokens), level_table.t...]
    reshape x1 -> x0, local copies, waits for them, and re-layouts: 0.77 us -> none  [per_device(): level_table.reshape(ntab, local_heads * levels)]
where the time goes in v2:
time: 41.4 us; the launch traced here: 41.1 us
  Pallas kernels  36.8 us (89%)
  local copies, waits for them, and re-layouts  3.74 us (9%)
  between operations  0.64 us (2%)
    pallas_call x1, Pallas kernels, per_device(): call(queries, keys, values, level_index.reshape(1, tokens), level_table.t...  36.8 us
    unnamed x2, local copies, waits for them, and re-layouts  3.74 us

profile of v2, /device:TPU:0, one launch (start us, length us, event | category | flops | bytes accessed | tf_op | source)
XLA Modules:
  0.0 41.1 jit_solution(7608711548609473557)
XLA Ops:
  0.6 36.8 %shard_map.122 = (bf16[256,1024]{1,0:T(8,128)(2,1)}, bf16[1024,256]{1,0:T(8,128)(2,1)}) custom-call(bf16[1024,256]{1,0:T(8,128)(2,1)} %q_hbm.1, bf16[1024,256]{1,0:T(8,128)(2,1)} %k_hbm.1, bf16[1024,256]{1,0:T(8,128)(2,1)} %v_hbm.1, s32[1,1024]{1,0:T(1,128)} %bitcast.7, f32[16,16]{1,0:T(8,128)} %bitcast.6, f32[1,256]{1,0:T(1,128)} %bitcast.9, ...), custom_call_target="tpu_custom_call" | custom-call | tf_op jit(solution)/shard_map/pallas_call | solution.py:488
  37.4 1.9 %copy.15 = bf16[256,1024]{1,0:T(8,128)(2,1)} copy(bf16[256,1024]{1,0:T(8,128)(2,1)} %get-tuple-element.4) | data formatting | bytes 1048576
  39.3 1.9 %copy.16 = bf16[1024,256]{1,0:T(8,128)(2,1)} copy(bf16[1024,256]{1,0:T(8,128)(2,1)} %get-tuple-element.5) | data formatting | bytes 1048576

commit v3 on v2

--- a/solution.py
+++ b/solution.py
@@ -9,6 +9,8 @@
 from jax.sharding import PartitionSpec as P
 
 STRETCH = 64
+STRETCH_BITS = 6
+PIECES = 4
 EPSILON = 1e-05
 VMEM_BYTES = 60 * 2**20
 MESH = pl.DeviceIdType.MESH
@@ -159,11 +161,21 @@
             device_id_type=MESH,
         )
 
-    def res_copy(slot, source, to):
-        src = res_hbm if slot <= hops else res_ref.at[source]
+    def res_copy(slot, p, source, to):
+        part = pl.ds(p * (rows // PIECES), rows // PIECES)
+        src = res_hbm.at[part] if slot <= hops else res_ref.at[source, part]
         return remote(
-            src, res_ref.at[source], res_send_sem.at[slot], res_recv_sem.at[slot], {"head": to}
+            src,
+            res_ref.at[source, part],
+            res_send_sem.at[slot, p],
+            res_recv_sem.at[slot, p],
+            {"head": to},
         )
+
+    def res_forward(p):
+        for j in range(1, hops + 1):
+            res_copy(j, p, behind(j), me).wait_recv()
+            res_copy(hops + j, p, behind(j), sib).start()
 
     def ho_copy(slot, c, source, to):
         block = ho_ref.at[source, c]
@@ -200,6 +212,11 @@
         for h in range(local_heads):
             read_ref[h, :, b * dim : (b + 1) * dim] = used[h * dim : (h + 1) * dim]
         cur_ref[...] += arrived.astype(F32)
+
+    for p in range(PIECES):
+        for j in range(1, hops + 1):
+            res_copy(j, p, me, ahead(j)).start()
+        res_copy(0, p, me, sib).start()
 
     load_k.wait()
     load_v.wait()
@@ -213,15 +230,13 @@
         states.append(mine)
         cur_ref[cols, :] = functools.reduce(lambda a, b: a + b, mine)
     state_start(0)
-    res_copy(0, me, sib).start()
-    for j in range(1, hops + 1):
-        res_copy(j, me, ahead(j)).start()
 
     for copy in small:
         copy.wait()
     columns = local_heads * levels
-    place = lax.broadcasted_iota(jnp.int32, (columns, 1), 0)
-    level = lax.rem(place, levels)
+    level = lax.broadcasted_iota(jnp.int32, (columns, 1), 0)
+    for h in range(local_heads - 1):
+        level = jnp.where(level >= levels, level - levels, level)
     rate = jnp.full((columns, 1), STRETCH ** (-0.5), F32)
     for b in range(1, levels - 1):
         rate = jnp.where(level == b + 1, (STRETCH * 2**b) ** (-0.5), rate)
@@ -232,12 +247,11 @@
     low = (rest - mid.astype(F32)).astype(BF16)
     row = lax.broadcasted_iota(jnp.int32, (columns, columns * dim), 0)
     lane = lax.broadcasted_iota(jnp.int32, (columns, columns * dim), 1)
-    spread = (lane // dim == row).astype(F32).astype(BF16)
+    spread = ((lane >= row * dim) & (lane < (row + 1) * dim)).astype(F32).astype(BF16)
     for i, term in enumerate((high, mid, low)):
         spread_ref[i * ntab : (i + 1) * ntab] = dot_tn(term, spread).astype(BF16)
 
-    entry = lax.broadcasted_iota(jnp.int32, (3 * ntab, rows), 0)
-    entry = lax.rem(entry, ntab)
+    entry = jnp.concatenate([lax.broadcasted_iota(jnp.int32, (ntab, rows), 0)] * 3, 0)
 
     def weights(offset, h, first, count):
         chosen = jnp.broadcast_to(index_ref[:, pl.ds(offset, rows)], (3 * ntab, rows))
@@ -252,8 +266,8 @@
     def near(c):
         offset = c * rows
         span = slice(offset, offset + rows)
-        tc = t // STRETCH
-        sc = s // STRETCH
+        tc = t >> STRETCH_BITS
+        sc = s >> STRETCH_BITS
         for h in range(local_heads):
             cols = slice(h * dim, (h + 1) * dim)
             w = weights(offset, h, 0, 1 + inner_bits + chunk_bits)
@@ -265,8 +279,7 @@
             scores = dot_nt(q, k_ref[span, cols])
             factor = jnp.where((tc == sc) & (s <= t), wide(0), 0.0)
             for b in range(inner_bits):
-                member = (sc // 2**b) == (tc // 2**b) - 1
-                member &= lax.rem(tc // 2**b, 2) == 1
+                member = ((sc >> b) == (tc >> b) - 1) & (((tc >> b) & 1) == 1)
                 factor = jnp.where(member, wide(1 + b), factor)
             out = dot((scores * factor).astype(BF16), v_ref[span, cols])
             for b in range(chunk_bits):
@@ -283,6 +296,8 @@
         if i < ctx_bits - 1:
             state_finish(i)
             state_start(i + 1)
+        if 1 <= i < 3:
+            res_forward(i - 1)
     for b in range(min(group, ctx_bits - 1), ctx_bits):
         state_finish(b)
         if b < ctx_bits - 1:
@@ -310,9 +325,8 @@
     lax.fori_loop(0, group, far, 0)
 
     load_res.wait()
-    for j in range(1, hops + 1):
-        res_copy(j, behind(j), me).wait_recv()
-        res_copy(hops + j, behind(j), sib).start()
+    for p in range(max(0, min(group, 3) - 1), PIECES):
+        res_forward(p)
     load_wo.wait()
     for copy in load_w3:
         copy.wait()
@@ -326,9 +340,10 @@
         return lax.rem(sib + group - 2 * j, group)
 
     forward(group - 1)
-    res_copy(0, sib, me).wait_recv()
-    for j in range(1, hops + 1):
-        res_copy(hops + j, forwarded(j), me).wait_recv()
+    for p in range(PIECES):
+        res_copy(0, p, sib, me).wait_recv()
+        for j in range(1, hops + 1):
+            res_copy(hops + j, p, forwarded(j), me).wait_recv()
 
     score_scale = dim ** (-0.5) * math.log2(math.e)
 
@@ -406,15 +421,38 @@
 
     for b in range(ctx_bits):
         state_copy(b).wait_send()
-    res_copy(0, me, sib).wait_send()
-    for j in range(1, hops + 1):
-        res_copy(j, me, ahead(j)).wait_send()
-        res_copy(hops + j, behind(j), sib).wait_send()
+    for p in range(PIECES):
+        res_copy(0, p, me, sib).wait_send()
+        for j in range(1, hops + 1):
+            res_copy(j, p, me, ahead(j)).wait_send()
+            res_copy(hops + j, p, behind(j), sib).wait_send()
     for c in range(group):
         ho_copy(0, c, me, sib).wait_send()
         for j in range(1, hops + 1):
             ho_copy(j, c, me, ahead(j)).wait_send()
             ho_copy(hops + j, c, behind(j), sib).wait_send()
+
+
+def hand_on(hidden_ref, attended_ref, hidden_out, attended_out, hidden_mid, attended_mid, sems):
+    moves = []
+    ways = ((hidden_ref, hidden_mid, hidden_out), (attended_ref, attended_mid, attended_out))
+    for src, mid, dst in ways:
+        part = src.shape[0] // PIECES
+        for p in range(PIECES):
+            span = pl.ds(p * part, part)
+            n = len(moves)
+            moves.append(
+                (
+                    pltpu.make_async_copy(src.at[span], mid.at[span], sems.at[0, n]),
+                    pltpu.make_async_copy(mid.at[span], dst.at[span], sems.at[1, n]),
+                )
+            )
+            moves[-1][0].start()
+    for first, second in moves:
+        first.wait()
+        second.start()
+    for first, second in moves:
+        second.wait()
 
 
 def per_device(
@@ -474,8 +512,8 @@
             dma((13,)),
             dma((ctx_bits,)),
             dma((ctx_bits,)),
-            dma((slots,)),
-            dma((slots,)),
+            dma((slots, PIECES)),
+            dma((slots, PIECES)),
             dma((slots, group)),
             dma((slots, group)),
             dma,
@@ -485,7 +523,7 @@
             collective_id=0, has_side_effects=True, vmem_limit_bytes=VMEM_BYTES
         ),
     )
-    return call(
+    hidden, attended = call(
         queries,
         keys,
         values,
@@ -498,6 +536,21 @@
         w_qkv,
         windows,
     )
+    return pl.pallas_call(
+        hand_on,
+        out_shape=(
+            jax.ShapeDtypeStruct(residual.shape, BF16),
+            jax.ShapeDtypeStruct(queries.shape, BF16),
+        ),
+        in_specs=[anywhere] * 2,
+        out_specs=(anywhere, anywhere),
+        scratch_shapes=[
+            pltpu.VMEM(residual.shape, BF16),
+            pltpu.VMEM(queries.shape, BF16),
+            dma((2, 2 * PIECES)),
+        ],
+        compiler_params=pltpu.CompilerParams(vmem_limit_bytes=VMEM_BYTES),
+    )(hidden, attended)
 
 
 def solution(mesh):

time: 41.4 us -> 39.8 us (0.961)
  local copies, waits for them, and re-layouts: 3.74 us -> 0 us
  Pallas kernels: 36.8 us -> 39 us
    unnamed x2 -> x0, local copies, waits for them, and re-layouts: 3.74 us -> none
    pallas_call x0 -> x1, Pallas kernels: none -> 2.09 us  [per_device(): pl.pallas_call(hand_on, out_shape=(jax.ShapeDtypeStruct(residual.shape, B...]
where the time goes in v3:
time: 39.8 us; the launch traced here: 39.7 us
  Pallas kernels  39 us (98%)
  between operations  0.64 us (2%)
    pallas_call x1, Pallas kernels, per_device(): call(queries, keys, values, level_index.reshape(1, tokens), level_table.t...  36.9 us
    pallas_call x1, Pallas kernels, per_device(): pl.pallas_call(hand_on, out_shape=(jax.ShapeDtypeStruct(residual.shape, B...  2.09 us

profile of v3, /device:TPU:0, one launch (start us, length us, event | category | flops | bytes accessed | tf_op | source)
XLA Modules:
  0.0 39.7 jit_solution(9522251808305335147)
XLA Ops:
  0.6 36.9 %shard_map.122 = (bf16[256,1024]{1,0:T(8,128)(2,1)}, bf16[1024,256]{1,0:T(8,128)(2,1)}) custom-call(bf16[1024,256]{1,0:T(8,128)(2,1)} %q_hbm.1, bf16[1024,256]{1,0:T(8,128)(2,1)} %k_hbm.1, bf16[1024,256]{1,0:T(8,128)(2,1)} %v_hbm.1, s32[1,1024]{1,0:T(1,128)} %bitcast.7, f32[16,16]{1,0:T(8,128)} %bitcast.6, f32[1,256]{1,0:T(1,128)} %bitcast.9, ...), custom_call_target="tpu_custom_call" | custom-call | tf_op jit(solution)/shard_map/pallas_call | solution.py:526
  37.6 2.1 %shard_map.123 = (bf16[256,1024]{1,0:T(8,128)(2,1)}, bf16[1024,256]{1,0:T(8,128)(2,1)}) custom-call(bf16[256,1024]{1,0:T(8,128)(2,1)} %get-tuple-element.4.hidden_ref, bf16[1024,256]{1,0:T(8,128)(2,1)} %get-tuple-element.5.attended_ref), custom_call_target="tpu_custom_call" | custom-call | tf_op jit(solution)/shard_map/pallas_call | solution.py:539
